TPU v7x, 256 devices: a whole 4x4x8 slice. The times are simulated.
256 devices in a mesh: bld: 32 (over x, z), tm: 8 (over y, core).
Axes of the slice: x: 4, y: 4, z: 8, core: 2. Of those that a mesh axis runs over, the one named last changes fastest.
Arguments:
- power: float32 [32768, 2048], P('bld', 'tm'), may hold values from 0.05 to 3.9, as said below
- base_temp: float32 [32768, 2048], P('bld', 'tm'), may hold values from -8 to 8
- band_low: float32 [8, 2048], P(None, 'tm'), may hold values from -1.2 to -0.3
- band_high: float32 [8, 2048], P(None, 'tm'), may hold values from 0.3 to 1.2
- kernels: bfloat16 [4, 256], replicated, as said below
- gains: float32 [32768, 4], P('bld'), may hold values from 0.3 to 3
- zones: int32 [32768], P('bld'), may hold values from 1 to 4
- plan_class: int32 [32768], P('bld'), may hold values from 0 to 7
- duals: float32 [2048], P('tm'), may hold values from -2 to 2
Outputs:
- power_out: float32 [32768, 2048], P('bld', 'tm')
- duals_out: float32 [2048], P('tm')
Inputs may be any that keep to these rules, and one draw needn't show every extreme that they name: power of a building lies between 0.05 and 3.9. Impulse kernels are nonnegative.
All inputs are finite; a program needn't handle non-finite values.
Results may differ from a plain program's by a relative error of at most 0.00069.
Values may be sent and summed in bfloat16 or wider, within the bound.
A program may use at most 64 MiB of HBM per device.

v0:
```python
import functools

import jax
import jax.numpy as jnp
from jax import lax
from jax.experimental import pallas as pl
from jax.experimental.pallas import tpu as pltpu
from jax.sharding import PartitionSpec as P

ITERS = 2
ROWS = 128
MESH = pl.DeviceIdType.MESH
CODE = 32767.0


def split3(value):
    top = value.astype(jnp.bfloat16)
    rest = value - top.astype(jnp.float32)
    mid = rest.astype(jnp.bfloat16)
    low = (rest - mid.astype(jnp.float32)).astype(jnp.bfloat16)
    return [top, mid, low]


def kernel(
    nz,
    nx,
    nt,
    power,
    base,
    band_low,
    band_high,
    kernels,
    gains,
    zones,
    classes,
    duals,
    out,
    duals_out,
    u_now,
    base_vm,
    over,
    under,
    own,
    packed,
    halo_u,
    code_out,
    code_in,
    forward,
    adjoint,
    bands,
    onehot,
    cols,
    sums,
    part_z,
    part_x,
    part_t,
    load_sem,
    u_send,
    u_recv,
    p_send,
    p_recv,
    r_send,
    r_recv,
):
    count, steps = u_now.shape
    zcount = kernels.shape[0]
    chunks = count // ROWS
    bld = lax.axis_index("bld")
    tm = lax.axis_index("tm")
    x, z = bld // nz, lax.rem(bld, nz)
    right = (bld, lax.rem(tm + 1, nt))
    left = (bld, lax.rem(tm + nt - 1, nt))
    peers_z = [(x * nz + lax.rem(z + k, nz), tm) for k in range(1, nz)]
    peers_x = [(lax.rem(x + k, nx) * nz + z, tm) for k in range(1, nx)]
    peers_t = [(bld, lax.rem(tm + k, nt)) for k in range(1, nt)]

    def rows(c):
        return pl.ds(pl.multiple_of(c * ROWS, ROWS), ROWS)

    def load(which, c):
        source, target = ((power, u_now), (base, base_vm))[which]
        return pltpu.make_async_copy(
            source.at[rows(c)], target.at[rows(c)], load_sem.at[which, c]
        )

    def u_copy(it, c):
        return pltpu.make_async_remote_copy(
            src_ref=packed.at[it, rows(c)],
            dst_ref=halo_u.at[it, rows(c)],
            send_sem=u_send.at[it, c],
            recv_sem=u_recv.at[it, c],
            device_id=right,
            device_id_type=MESH,
        )

    def p_copy(it, c):
        return pltpu.make_async_remote_copy(
            src_ref=code_out.at[it, rows(c)],
            dst_ref=code_in.at[it, rows(c)],
            send_sem=p_send.at[it, c],
            recv_sem=p_recv.at[it, c],
            device_id=left,
            device_id_type=MESH,
        )

    stages = ((part_z, peers_z, z, 0), (part_x, peers_x, x, nz), (part_t, peers_t, tm, nz + nx))

    def part_copy(it, stage, k):
        buf, peers, mine, first = stages[stage]
        return pltpu.make_async_remote_copy(
            src_ref=buf.at[it, mine],
            dst_ref=buf.at[it, mine],
            send_sem=r_send.at[it, first + k],
            recv_sem=r_recv.at[it, first + k],
            device_id=peers[k - 1],
            device_id_type=MESH,
        )

    def stage_send(it, stage, value):
        buf, peers, mine, _ = stages[stage]
        buf[it, mine] = value
        for k in range(1, len(peers) + 1):
            part_copy(it, stage, k).start()

    def stage_wait(it, stage):
        buf, peers, _, _ = stages[stage]
        for k in range(1, len(peers) + 1):
            part_copy(it, stage, k).wait_recv()
        return buf[it]

    def send_local(it):
        stage_send(it, 0, jnp.sum(sums[it], axis=0, keepdims=True))

    def send_rows(it):
        stage_send(it, 1, jnp.sum(stage_wait(it, 0), axis=0))

    def send_peak(it):
        fleet = jnp.sum(stage_wait(it, 1), axis=0)
        top = jnp.max(fleet, axis=1, keepdims=True)
        stage_send(it, 2, jnp.broadcast_to(top, (1, 128)))

    def ratio(it):
        fleet = jnp.sum(part_x[it], axis=0)
        top = jnp.max(stage_wait(it, 2), axis=0)[:, :1]
        return fleet / top

    for c in range(chunks):
        load(0, c).start()
    for c in range(chunks):
        load(1, c).start()

    barrier = pltpu.get_barrier_semaphore()
    for peer in peers_z + peers_x + peers_t:
        pl.semaphore_signal(barrier, inc=1, device_id=peer, device_id_type=MESH)

    sums[...] = jnp.zeros_like(sums)

    def pack(c, carry):
        load(0, c).wait()
        value = u_now[rows(c)]
        packed[0, rows(c)] = value.astype(jnp.bfloat16)
        sums[0] += jnp.sum(value.reshape(ROWS // 8, 8, steps), axis=0)
        return carry

    lax.fori_loop(0, chunks, pack, 0)
    pl.semaphore_wait(barrier, len(peers_z + peers_x + peers_t))
    send_local(0)

    def send_first(c, carry):
        u_copy(0, c).start()
        return carry

    lax.fori_loop(0, chunks, send_first, 0)

    kern = kernels[...].astype(jnp.float32)
    at_row = lax.broadcasted_iota(jnp.int32, (steps, steps), 0)
    at_col = lax.broadcasted_iota(jnp.int32, (steps, steps), 1)
    edge = jnp.where(tm > 0, 0, steps)
    for slot in range(zcount):
        wide = jnp.broadcast_to(kern[slot : slot + 1], (steps, steps))
        ring = pltpu.roll(wide, 0, 1, stride=1, stride_axis=0)
        place = pl.ds(slot * steps, steps)
        forward[:steps, place] = jnp.where(at_row - at_col > edge, ring, 0.0).astype(jnp.bfloat16)
        forward[steps:, place] = jnp.where(at_row <= at_col, ring, 0.0).astype(jnp.bfloat16)
        ring = ring.T
        adjoint[place, :steps] = jnp.where(at_row >= at_col, ring, 0.0).astype(jnp.bfloat16)
        adjoint[place, steps:] = jnp.where(at_col - at_row > edge, ring, 0.0).astype(jnp.bfloat16)

    gain = gains[...]
    slots = lax.broadcasted_iota(jnp.int32, (zcount, count), 0)
    weight = jnp.where(slots < zones[...], gain, 0.0)
    total = jnp.sum(kern, axis=1, keepdims=True)
    bound = 1.01 * jnp.sum(weight * total * (8.0 + 4.0 * gain * total), axis=0, keepdims=True)
    bound = jnp.maximum(bound, 1e-20)
    scale_in = bound / (CODE * CODE)
    scale_out = (CODE * CODE) / bound
    none = jnp.zeros((6, count), jnp.float32)
    cols[...] = jnp.concatenate([gain, weight, scale_out, scale_in, none], axis=0).T
    nsched = band_low.shape[0]
    plans = lax.broadcasted_iota(jnp.int32, (nsched, count), 0)
    chosen = jnp.where(plans == classes[...], 1.0, 0.0)
    onehot[...] = jnp.concatenate([chosen] * 3, axis=0).T.astype(jnp.bfloat16)
    lows, highs = split3(band_low[...]), split3(band_high[...])
    bands[...] = jnp.concatenate(
        [jnp.concatenate([lo, hi], axis=1).astype(jnp.float32) for lo, hi in zip(lows, highs)],
        axis=0,
    ).astype(jnp.bfloat16)

    def excess_and_pull(it, c):
        col = cols[rows(c)]
        window = jnp.concatenate([halo_u[it, rows(c)], packed[it, rows(c)]], axis=1)
        hi, lo = over[rows(c)], under[rows(c)]
        parts = []
        for slot in range(zcount):
            place = pl.ds(slot * steps, steps)
            response = jnp.dot(window, forward[:, place], preferred_element_type=jnp.float32)
            change = col[:, slot : slot + 1] * response
            far = jnp.maximum(hi - change, jnp.minimum(lo - change, 0.0))
            scale = col[:, zcount + slot : zcount + slot + 1]
            parts.append((scale * far).astype(jnp.bfloat16))
        excess = jnp.concatenate(parts, axis=1)
        pull = jnp.dot(excess, adjoint[...], preferred_element_type=jnp.float32)
        own[rows(c)] = pull[:, :steps]
        sent = pull[:, steps:]
        size = jnp.sqrt(jnp.abs(sent) * col[:, 2 * zcount : 2 * zcount + 1])
        code = jnp.round(jnp.where(sent < 0.0, -size, size))
        code_out[it, rows(c)] = jnp.clip(code, -CODE, CODE).astype(jnp.int16)

    def updated(it, c, price):
        p_copy(it, c).wait_recv()
        code = code_in[it, rows(c)].astype(jnp.float32)
        scale = cols[rows(c)][:, 2 * zcount + 1 : 2 * zcount + 2]
        pull = own[rows(c)] + code * jnp.abs(code) * scale
        return jnp.clip(u_now[rows(c)] - 0.5 * (price - pull), 0.0, 4.0)

    def first(c):
        load(1, c).wait()
        limits = jnp.dot(onehot[rows(c)], bands[...], preferred_element_type=jnp.float32)
        value = base_vm[rows(c)]
        under[rows(c)] = value - limits[:, :steps]
        over[rows(c)] = value - limits[:, steps:]
        u_copy(0, c).wait_recv()
        excess_and_pull(0, c)
        p_copy(0, c).start()

    def second(c):
        u_copy(1, c).wait_recv()
        excess_and_pull(1, c)
        p_copy(1, c).start()

    def between(c, price):
        value = updated(0, c, price)
        u_now[rows(c)] = value
        packed[1, rows(c)] = value.astype(jnp.bfloat16)
        sums[1] += jnp.sum(value.reshape(ROWS // 8, 8, steps), axis=0)
        u_copy(1, c).start()

    send_rows(0)
    first(0)
    send_peak(0)
    first(1)
    now = ratio(0)
    price = duals[...] + 1.0 * now
    y_now = duals[...] + 1.0 * (now - 0.5)

    def middle(c, carry):
        first(c)
        between(c - 2, price)
        return carry

    lax.fori_loop(2, chunks, middle, 0)
    between(chunks - 2, price)
    between(chunks - 1, price)
    send_local(1)
    second(0)
    send_rows(1)
    second(1)
    send_peak(1)

    def last(c, carry):
        second(c)
        return carry

    lax.fori_loop(2, chunks, last, 0)
    now = ratio(1)
    price = y_now + 1.0 * now
    duals_out[...] = y_now + 1.0 * (now - 0.5)

    def finish(c, carry):
        out[rows(c)] = updated(1, c, price)
        return carry

    lax.fori_loop(0, chunks, finish, 0)

    for it in range(ITERS):
        for c in range(chunks):
            u_copy(it, c).wait_send()
            p_copy(it, c).wait_send()
        for stage in range(3):
            for k in range(1, len(stages[stage][1]) + 1):
                part_copy(it, stage, k).wait_send()


def body(nz, nx, nt, power, base, band_low, band_high, kernels, gains, zones, classes, duals):
    count, steps = power.shape
    zcount = kernels.shape[0]
    chunks = count // ROWS
    nsched = band_low.shape[0]
    vmem = pl.BlockSpec(memory_space=pltpu.VMEM)
    anywhere = pl.BlockSpec(memory_space=pl.ANY)
    f32, bf16 = jnp.float32, jnp.bfloat16
    whole = pltpu.VMEM((count, steps), f32)
    parts = nz + nx + nt
    out, duals_out = pl.pallas_call(
        functools.partial(kernel, nz, nx, nt),
        out_shape=(
            jax.ShapeDtypeStruct((count, steps), f32),
            jax.ShapeDtypeStruct((1, steps), f32),
        ),
        in_specs=[anywhere] * 2 + [vmem] * 7,
        out_specs=(vmem, vmem),
        scratch_shapes=[
            whole,
            whole,
            whole,
            whole,
            whole,
            pltpu.VMEM((ITERS, count, steps), bf16),
            pltpu.VMEM((ITERS, count, steps), bf16),
            pltpu.VMEM((ITERS, count, steps), jnp.int16),
            pltpu.VMEM((ITERS, count, steps), jnp.int16),
            pltpu.VMEM((2 * steps, zcount * steps), bf16),
            pltpu.VMEM((zcount * steps, 2 * steps), bf16),
            pltpu.VMEM((3 * nsched, 2 * steps), bf16),
            pltpu.VMEM((count, 3 * nsched), bf16),
            pltpu.VMEM((count, 16), f32),
            pltpu.VMEM((ITERS, 8, steps), f32),
            pltpu.VMEM((ITERS, nz, 1, steps), f32),
            pltpu.VMEM((ITERS, nx, 1, steps), f32),
            pltpu.VMEM((ITERS, nt, 1, 128), f32),
            pltpu.SemaphoreType.DMA((2, chunks)),
            pltpu.SemaphoreType.DMA((ITERS, chunks)),
            pltpu.SemaphoreType.DMA((ITERS, chunks)),
            pltpu.SemaphoreType.DMA((ITERS, chunks)),
            pltpu.SemaphoreType.DMA((ITERS, chunks)),
            pltpu.SemaphoreType.DMA((ITERS, parts)),
            pltpu.SemaphoreType.DMA((ITERS, parts)),
        ],
        compiler_params=pltpu.CompilerParams(
            collective_id=0, has_side_effects=True, vmem_limit_bytes=40 * 1024 * 1024
        ),
    )(
        power,
        base,
        band_low,
        band_high,
        kernels,
        gains.T,
        zones[None, :],
        classes[None, :],
        duals[None, :],
    )
    return out, duals_out[0]


def solution(mesh):
    in_specs = (
        P("bld", "tm"),
        P("bld", "tm"),
        P(None, "tm"),
        P(None, "tm"),
        P(),
        P("bld", None),
        P("bld"),
        P("bld"),
        P("tm"),
    )
    out_specs = (P("bld", "tm"), P("tm"))
    nz = 8 if mesh.shape["bld"] % 8 == 0 else 1
    nx = mesh.shape["bld"] // nz
    return jax.shard_map(
        functools.partial(body, nz, nx, mesh.shape["tm"]),
        mesh=mesh,
        in_specs=in_specs,
        out_specs=out_specs,
        check_vma=False,
    )
```

profile of v0, /device:TPU:1, one launch (start us, length us, event | category | flops | bytes accessed | tf_op | source)
XLA Modules:
  0.0 55.9 jit_solution(11364270119822638585)
XLA Ops:
  0.6 0.0 copy-start.5
  0.6 0.0 copy-start.7
  0.7 0.0 copy-start.8
  0.7 0.7 %copy-done.5 = s32[1024]{0:T(1024)S(1)} copy-done((s32[1024]{0:T(1024)S(1)}, s32[1024]{0:T(1024)}, u32[]{:S(2)}) %copy-start.5) | copy-done | bytes 4120
  1.3 0.0 copy-done.7
  1.3 0.0 copy-done.8
  1.3 0.0 copy-start
  1.3 1.2 %copy-done = f32[1024,256]{1,0:T(8,128)S(1)} copy-done((f32[1024,256]{1,0:T(8,128)S(1)}, f32[1024,256]{1,0:T(8,128)}, u32[]{:S(2)}) %copy-start) | copy-done | bytes 1048600
  2.6 0.0 copy-start.1
  2.6 1.2 %copy-done.1 = f32[1024,256]{1,0:T(8,128)S(1)} copy-done((f32[1024,256]{1,0:T(8,128)S(1)}, f32[1024,256]{1,0:T(8,128)}, u32[]{:S(2)}) %copy-start.1) | copy-done | bytes 1048600
  3.8 0.0 copy-start.2
  3.8 0.7 %copy-done.2 = f32[1024,4]{0,1:T(4,128)S(1)} copy-done((f32[1024,4]{0,1:T(4,128)S(1)}, f32[1024,4]{0,1:T(4,128)}, u32[]{:S(2)}) %copy-start.2) | copy-done | bytes 16408
  4.5 0.0 copy-start.3
  4.5 0.7 %copy-done.3 = f32[8,256]{1,0:T(8,128)S(1)} copy-done((f32[8,256]{1,0:T(8,128)S(1)}, f32[8,256]{1,0:T(8,128)}, u32[]{:S(2)}) %copy-start.3) | copy-done | bytes 8216
  5.2 0.0 copy-start.4
  5.2 0.7 %copy-done.4 = f32[8,256]{1,0:T(8,128)S(1)} copy-done((f32[8,256]{1,0:T(8,128)S(1)}, f32[8,256]{1,0:T(8,128)}, u32[]{:S(2)}) %copy-start.4) | copy-done | bytes 8216
  5.9 0.0 copy-start.6
  5.9 0.7 %copy-done.6 = s32[1024]{0:T(1024)S(1)} copy-done((s32[1024]{0:T(1024)S(1)}, s32[1024]{0:T(1024)}, u32[]{:S(2)}) %copy-start.6) | copy-done | bytes 4120
  6.6 47.8 %shard_map.104 = (f32[1024,256]{1,0:T(8,128)S(1)}, f32[1,256]{1,0:T(1,128)S(1)}) custom-call(f32[1024,256]{1,0:T(8,128)S(1)} %copy-done, f32[1024,256]{1,0:T(8,128)S(1)} %copy-done.1, f32[8,256]{1,0:T(8,128)S(1)} %copy-done.3, f32[8,256]{1,0:T(8,128)S(1)} %copy-done.4, bf16[4,256]{1,0:T(4,128)(2,1)S(1)} %copy-done.7, f32[4,1024]{1,0:T(4,128)S(1)} %bitcast.5, ...), custom_call_target="tpu_custom_call" | custom-call | tf_op jit(solution)/shard_map/pallas_call | solution.py:314
  54.4 1.0 %copy.13 = f32[1024,256]{1,0:T(8,128)} copy(f32[1024,256]{1,0:T(8,128)S(1)} %get-tuple-element.8) | data formatting | bytes 2097152
  55.4 0.6 %copy.14 = f32[256]{0:T(256)} copy(f32[256]{0:T(256)S(1)} %bitcast.9) | data formatting | bytes 2048
Async XLA Ops:
  0.6 0.7 %copy-start.5 = (s32[1024]{0:T(1024)S(1)}, s32[1024]{0:T(1024)}, u32[]{:S(2)}) copy-start(s32[1024]{0:T(1024)} %param.15) | copy-start | bytes 12292
  0.6 0.7 %copy-start.7 = (bf16[4,256]{1,0:T(4,128)(2,1)S(1)}, bf16[4,256]{1,0:T(4,128)(2,1)}, u32[]{:S(2)}) copy-start(bf16[4,256]{1,0:T(4,128)(2,1)} %kernels.1) | copy-start | bytes 6148
  0.7 0.7 %copy-start.8 = (f32[256]{0:T(256)S(1)}, f32[256]{0:T(256)}, u32[]{:S(2)}) copy-start(f32[256]{0:T(256)} %param.17) | copy-start | bytes 3076
  1.3 1.2 %copy-start = (f32[1024,256]{1,0:T(8,128)S(1)}, f32[1024,256]{1,0:T(8,128)}, u32[]{:S(2)}) copy-start(f32[1024,256]{1,0:T(8,128)} %power.1) | copy-start | bytes 3145732
  2.6 1.2 %copy-start.1 = (f32[1024,256]{1,0:T(8,128)S(1)}, f32[1024,256]{1,0:T(8,128)}, u32[]{:S(2)}) copy-start(f32[1024,256]{1,0:T(8,128)} %base.1) | copy-start | bytes 3145732
  3.8 0.7 %copy-start.2 = (f32[1024,4]{0,1:T(4,128)S(1)}, f32[1024,4]{0,1:T(4,128)}, u32[]{:S(2)}) copy-start(f32[1024,4]{0,1:T(4,128)} %param.14) | copy-start | bytes 49156
  4.5 0.7 %copy-start.3 = (f32[8,256]{1,0:T(8,128)S(1)}, f32[8,256]{1,0:T(8,128)}, u32[]{:S(2)}) copy-start(f32[8,256]{1,0:T(8,128)} %band_low.1) | copy-start | bytes 24580
  5.2 0.7 %copy-start.4 = (f32[8,256]{1,0:T(8,128)S(1)}, f32[8,256]{1,0:T(8,128)}, u32[]{:S(2)}) copy-start(f32[8,256]{1,0:T(8,128)} %band_high.1) | copy-start | bytes 24580
  5.9 0.7 %copy-start.6 = (s32[1024]{0:T(1024)S(1)}, s32[1024]{0:T(1024)}, u32[]{:S(2)}) copy-start(s32[1024]{0:T(1024)} %param.16) | copy-start | bytes 12292
where the time goes:
time: 56.3 us; the launch traced here: 55.9 us
  Pallas kernels  47.8 us (85%)
  local copies, waits for them, and re-layouts  7.47 us (13%)
  between operations  0.67 us (1%)
    pallas_call x1, Pallas kernels, body(): pl.pallas_call(functools.partial(kernel, nz, nx, nt), out_shape=(jax.Shap...  47.8 us
    unnamed x20, local copies, waits for them, and re-layouts  7.47 us

commit v1 on v0

v1 whole, which is shorter than its diff:
```python
import functools

import jax
import jax.numpy as jnp
from jax import lax
from jax.experimental import pallas as pl
from jax.experimental.pallas import tpu as pltpu
from jax.sharding import PartitionSpec as P

ITERS = 2
ROWS = 128
MESH = pl.DeviceIdType.MESH
CODE = 32767.0


def split3(value):
    top = value.astype(jnp.bfloat16)
    rest = value - top.astype(jnp.float32)
    mid = rest.astype(jnp.bfloat16)
    low = (rest - mid.astype(jnp.float32)).astype(jnp.bfloat16)
    return [top, mid, low]


def spread(distances):
    return sorted(range(1, len(distances)), key=lambda k: -distances[k])


def around(k, n):
    return min(k, n - k)


def kernel(
    nz,
    nx,
    nt,
    power,
    base,
    band_low,
    band_high,
    kernels,
    gains,
    zones,
    classes,
    duals,
    out,
    duals_out,
    low_vm,
    high_vm,
    kern_vm,
    gains_vm,
    zones_vm,
    classes_vm,
    duals_vm,
    u_now,
    over,
    under,
    own,
    packed,
    halo_u,
    code_out,
    code_in,
    forward,
    adjoint,
    onehot,
    cols,
    part_a,
    part_b,
    load_sem,
    u_send,
    u_recv,
    p_send,
    p_recv,
    r_send,
    r_recv,
):
    count, steps = u_now.shape
    zcount = kernels.shape[0]
    copies = count // ROWS
    ny = nt // 2
    bld = lax.axis_index("bld")
    tm = lax.axis_index("tm")
    x, z = bld // nz, lax.rem(bld, nz)
    y, core = tm // 2, lax.rem(tm, 2)
    right = (bld, lax.rem(tm + 1, nt))
    left = (bld, lax.rem(tm + nt - 1, nt))

    far_a = spread([2 * around(k // 2, nz) + k % 2 for k in range(2 * nz)])
    far_b = spread([around(k // ny, nx) + around(k % ny, ny) for k in range(nx * ny)])
    peers_a = [
        (x * nz + lax.rem(z + k // 2, nz), 2 * y + lax.rem(core + k % 2, 2)) for k in far_a
    ]
    peers_b = [
        (lax.rem(x + k // ny, nx) * nz + z, 2 * lax.rem(y + k % ny, ny) + core) for k in far_b
    ]
    stages = ((part_a, peers_a, 2 * z + core), (part_b, peers_b, x * ny + y))

    small = (
        (gains, gains_vm),
        (zones, zones_vm),
        (classes, classes_vm),
        (kernels, kern_vm),
        (band_low, low_vm),
        (band_high, high_vm),
        (duals, duals_vm),
    )
    half = count // 2
    loads = [
        pltpu.make_async_copy(power.at[pl.ds(0, half)], u_now.at[pl.ds(0, half)], load_sem.at[0]),
        pltpu.make_async_copy(power.at[pl.ds(half, half)], u_now.at[pl.ds(half, half)], load_sem.at[1]),
        pltpu.make_async_copy(base, under, load_sem.at[2]),
    ] + [
        pltpu.make_async_copy(source, target, load_sem.at[3 + i])
        for i, (source, target) in enumerate(small)
    ]

    def u_copy(it, at, size):
        return pltpu.make_async_remote_copy(
            src_ref=packed.at[it, pl.ds(at, size)],
            dst_ref=halo_u.at[it, pl.ds(at, size)],
            send_sem=u_send.at[it],
            recv_sem=u_recv.at[it, at // ROWS],
            device_id=right,
            device_id_type=MESH,
        )

    def p_copy(it, at, size):
        return pltpu.make_async_remote_copy(
            src_ref=code_out.at[it, pl.ds(at, size)],
            dst_ref=code_in.at[it, pl.ds(at, size)],
            send_sem=p_send.at[it],
            recv_sem=p_recv.at[it, at // ROWS],
            device_id=left,
            device_id_type=MESH,
        )

    def part_send(it, stage, value):
        buf, peers, mine = stages[stage]
        buf[it, mine] = value
        for peer in peers:
            pltpu.make_async_remote_copy(
                src_ref=buf.at[it, mine],
                dst_ref=buf.at[it, mine],
                send_sem=r_send.at[it, stage],
                recv_sem=r_recv.at[it, stage],
                device_id=peer,
                device_id_type=MESH,
            ).start()

    def part_all(it, stage):
        buf, peers, _ = stages[stage]
        return pltpu.make_async_remote_copy(
            src_ref=buf.at[it, pl.ds(0, len(peers))],
            dst_ref=buf.at[it, pl.ds(0, len(peers))],
            send_sem=r_send.at[it, stage],
            recv_sem=r_recv.at[it, stage],
            device_id=peers[0],
            device_id_type=MESH,
        )

    def send_local(it, sums):
        part_send(it, 0, jnp.sum(sums, axis=0, keepdims=True))

    def send_pair(it):
        part_all(it, 0).wait_recv()
        slots = part_a[it].reshape(nz, 2, 1, steps)
        part_send(it, 1, jnp.sum(slots, axis=0))

    def ratio(it):
        part_all(it, 1).wait_recv()
        fleet = jnp.sum(part_b[it].reshape(nx, ny, 2, steps), axis=0)
        top = jnp.max(fleet, axis=(0, 1, 2), keepdims=True)[0, 0]
        mine = part_b[it, y, core]
        for k in range(1, nx):
            mine = mine + part_b[it, k * ny + y, core]
        return mine / top

    for load in loads:
        load.start()

    barrier = pltpu.get_barrier_semaphore()
    others = peers_a + peers_b + [left, right]
    for peer in others:
        pl.semaphore_signal(barrier, inc=1, device_id=peer, device_id_type=MESH)

    def fold(value):
        return jnp.sum(value.reshape(value.shape[0] // 8, 8, steps), axis=0)

    sums = jnp.zeros((8, steps), jnp.float32)
    for i in range(2):
        loads[i].wait()
        value = u_now[pl.ds(i * half, half)]
        packed[0, pl.ds(i * half, half)] = value.astype(jnp.bfloat16)
        sums = sums + fold(value)
    sums_first = sums
    for load in loads[3:]:
        load.wait()

    kern = kern_vm[...].astype(jnp.float32)
    gain = gains_vm[...]
    slots = lax.broadcasted_iota(jnp.int32, (zcount, count), 0)
    weight = jnp.where(slots < zones_vm[...], gain, 0.0)
    total = jnp.sum(kern, axis=1, keepdims=True)
    bound = 1.01 * jnp.sum(weight * total * (8.0 + 4.0 * gain * total), axis=0, keepdims=True)
    bound = jnp.maximum(bound, 1e-20)
    scale_in = bound / (CODE * CODE)
    scale_out = (CODE * CODE) / bound
    none = jnp.zeros((6, count), jnp.float32)
    cols[...] = jnp.concatenate([gain, weight, scale_out, scale_in, none], axis=0).T
    nsched = band_low.shape[0]
    plans = lax.broadcasted_iota(jnp.int32, (nsched, count), 0)
    chosen = jnp.where(plans == classes_vm[...], 1.0, 0.0)
    onehot[...] = jnp.concatenate([chosen] * 3, axis=0).T.astype(jnp.bfloat16)

    pl.semaphore_wait(barrier, len(others))
    send_local(0, sums_first)
    for at in range(0, count, ROWS):
        u_copy(0, at, ROWS).start()

    at_row = lax.broadcasted_iota(jnp.int32, (steps, steps), 0)
    at_col = lax.broadcasted_iota(jnp.int32, (steps, steps), 1)
    edge = jnp.where(tm > 0, 0, steps)
    for slot in range(zcount):
        wide = jnp.broadcast_to(kern[slot : slot + 1], (steps, steps))
        ring = pltpu.roll(wide, 0, 1, stride=1, stride_axis=0)
        place = pl.ds(slot * steps, steps)
        forward[:steps, place] = jnp.where(at_row - at_col > edge, ring, 0.0).astype(jnp.bfloat16)
        forward[steps:, place] = jnp.where(at_row <= at_col, ring, 0.0).astype(jnp.bfloat16)
        ring = ring.T
        adjoint[place, :steps] = jnp.where(at_row >= at_col, ring, 0.0).astype(jnp.bfloat16)
        adjoint[place, steps:] = jnp.where(at_col - at_row > edge, ring, 0.0).astype(jnp.bfloat16)

    lows, highs = split3(low_vm[...]), split3(high_vm[...])
    bands = jnp.concatenate(
        [jnp.concatenate([lo, hi], axis=1).astype(jnp.float32) for lo, hi in zip(lows, highs)],
        axis=0,
    ).astype(jnp.bfloat16)
    loads[2].wait()
    for at in range(0, count, half):
        rows = pl.ds(at, half)
        limits = jnp.dot(onehot[rows], bands, preferred_element_type=jnp.float32)
        value = under[rows]
        under[rows] = value - limits[:, :steps]
        over[rows] = value - limits[:, steps:]

    def excess_and_pull(it, at, size):
        for part in range(at, at + size, ROWS):
            u_copy(it, part, ROWS).wait_recv()
        rows = pl.ds(at, size)
        col = cols[rows]
        window = jnp.concatenate([halo_u[it, rows], packed[it, rows]], axis=1)
        hi, lo = over[rows], under[rows]
        parts = []
        for slot in range(zcount):
            place = pl.ds(slot * steps, steps)
            response = jnp.dot(window, forward[:, place], preferred_element_type=jnp.float32)
            change = col[:, slot : slot + 1] * response
            far = jnp.maximum(hi - change, jnp.minimum(lo - change, 0.0))
            scale = col[:, zcount + slot : zcount + slot + 1]
            parts.append((scale * far).astype(jnp.bfloat16))
        excess = jnp.concatenate(parts, axis=1)
        pull = jnp.dot(excess, adjoint[...], preferred_element_type=jnp.float32)
        own[rows] = pull[:, :steps]
        sent = pull[:, steps:]
        length = jnp.sqrt(jnp.abs(sent) * col[:, 2 * zcount : 2 * zcount + 1])
        code = jnp.round(jnp.where(sent < 0.0, -length, length))
        code_out[it, rows] = jnp.clip(code, -CODE, CODE).astype(jnp.int16)
        for part in range(at, at + size, ROWS):
            p_copy(it, part, ROWS).start()

    def free_part(it, at, size, y_now):
        for part in range(at, at + size, ROWS):
            p_copy(it, part, ROWS).wait_recv()
        rows = pl.ds(at, size)
        code = code_in[it, rows].astype(jnp.float32)
        scale = cols[rows][:, 2 * zcount + 1 : 2 * zcount + 2]
        pull = own[rows] + code * jnp.abs(code) * scale
        return u_now[rows] - 0.5 * (y_now - pull)

    y_now = duals_vm[...]
    places = [(0, 256), (256, 256), (512, 256), (768, 128), (896, 128)]
    assert places[-1][0] + places[-1][1] == count

    excess_and_pull(0, *places[0])
    send_pair(0)
    for place in places[1:]:
        excess_and_pull(0, *place)
    now = ratio(0)
    share = 0.5 * now
    sums = jnp.zeros((8, steps), jnp.float32)
    for at in range(0, count, ROWS):
        rows = pl.ds(at, ROWS)
        value = jnp.clip(free_part(0, at, ROWS, y_now) - share, 0.0, 4.0)
        u_now[rows] = value
        packed[1, rows] = value.astype(jnp.bfloat16)
        sums = sums + fold(value)
        u_copy(1, at, ROWS).start()
    send_local(1, sums)
    y_now = y_now + 1.0 * (now - 0.5)

    excess_and_pull(1, *places[0])
    excess_and_pull(1, *places[1])
    send_pair(1)
    for place in places[2:]:
        excess_and_pull(1, *place)
    for at, size in places:
        own[pl.ds(at, size)] = free_part(1, at, size, y_now)
    now = ratio(1)
    share = 0.5 * now
    duals_out[...] = y_now + 1.0 * (now - 0.5)
    out[...] = jnp.clip(own[...] - share, 0.0, 4.0)

    for it in range(ITERS):
        u_copy(it, 0, count).wait_send()
        p_copy(it, 0, count).wait_send()
        for stage in range(2):
            part_all(it, stage).wait_send()


def body(nz, nx, nt, power, base, band_low, band_high, kernels, gains, zones, classes, duals):
    count, steps = power.shape
    zcount = kernels.shape[0]
    copies = count // ROWS
    nsched = band_low.shape[0]
    vmem = pl.BlockSpec(memory_space=pltpu.VMEM)
    hbm = pl.BlockSpec(memory_space=pltpu.HBM)
    f32, bf16 = jnp.float32, jnp.bfloat16
    whole = pltpu.VMEM((count, steps), f32)
    args = (
        power,
        base,
        band_low,
        band_high,
        kernels,
        gains.T,
        zones[None, :],
        classes[None, :],
        duals[None, :],
    )
    out, duals_out = pl.pallas_call(
        functools.partial(kernel, nz, nx, nt),
        out_shape=(
            jax.ShapeDtypeStruct((count, steps), f32),
            jax.ShapeDtypeStruct((1, steps), f32),
        ),
        in_specs=[hbm] * len(args),
        out_specs=(vmem, vmem),
        scratch_shapes=[pltpu.VMEM(arg.shape, arg.dtype) for arg in args[2:]]
        + [
            whole,
            whole,
            whole,
            whole,
            pltpu.VMEM((ITERS, count, steps), bf16),
            pltpu.VMEM((ITERS, count, steps), bf16),
            pltpu.VMEM((ITERS, count, steps), jnp.int16),
            pltpu.VMEM((ITERS, count, steps), jnp.int16),
            pltpu.VMEM((2 * steps, zcount * steps), bf16),
            pltpu.VMEM((zcount * steps, 2 * steps), bf16),
            pltpu.VMEM((count, 3 * nsched), bf16),
            pltpu.VMEM((count, 16), f32),
            pltpu.VMEM((ITERS, 2 * nz, 1, steps), f32),
            pltpu.VMEM((ITERS, nx * nt // 2, 2, 1, steps), f32),
            pltpu.SemaphoreType.DMA((3 + len(args) - 2,)),
            pltpu.SemaphoreType.DMA((ITERS,)),
            pltpu.SemaphoreType.DMA((ITERS, copies)),
            pltpu.SemaphoreType.DMA((ITERS,)),
            pltpu.SemaphoreType.DMA((ITERS, copies)),
            pltpu.SemaphoreType.DMA((ITERS, 2)),
            pltpu.SemaphoreType.DMA((ITERS, 2)),
        ],
        compiler_params=pltpu.CompilerParams(
            collective_id=0, has_side_effects=True, vmem_limit_bytes=40 * 1024 * 1024
        ),
    )(*[pltpu.with_memory_space_constraint(arg, pltpu.HBM) for arg in args])
    return out, duals_out[0]


def solution(mesh):
    in_specs = (
        P("bld", "tm"),
        P("bld", "tm"),
        P(None, "tm"),
        P(None, "tm"),
        P(),
        P("bld", None),
        P("bld"),
        P("bld"),
        P("tm"),
    )
    out_specs = (P("bld", "tm"), P("tm"))
    nz = 8 if mesh.shape["bld"] % 8 == 0 else 1
    nx = mesh.shape["bld"] // nz
    return jax.shard_map(
        functools.partial(body, nz, nx, mesh.shape["tm"]),
        mesh=mesh,
        in_specs=in_specs,
        out_specs=out_specs,
        check_vma=False,
    )
```

time: 56.3 us -> 36.5 us (0.65)
  Pallas kernels: 47.8 us -> 34.3 us
  local copies, waits for them, and re-layouts: 7.47 us -> 1.54 us
    pallas_call x1, Pallas kernels: 47.8 us -> 34.3 us  [body(): pl.pallas_call(functools.partial(kernel, nz, nx, nt), out_shape=(jax.Shap...]
    unnamed x20 -> x2, local copies, waits for them, and re-layouts: 7.47 us -> 1.54 us
where the time goes in v1:
time: 36.5 us; the launch traced here: 36.4 us
  Pallas kernels  34.3 us (94%)
  local copies, waits for them, and re-layouts  1.54 us (4%)
  between operations  0.64 us (2%)
    pallas_call x1, Pallas kernels, body(): pl.pallas_call(functools.partial(kernel, nz, nx, nt), out_shape=(jax.Shap...  34.3 us
    unnamed x2, local copies, waits for them, and re-layouts  1.54 us

profile of v1, /device:TPU:1, one launch (start us, length us, event | category | flops | bytes accessed | tf_op | source)
XLA Modules:
  0.0 36.4 jit_solution(16302774789343982630)
XLA Ops:
  0.6 34.3 %shard_map.104 = (f32[1024,256]{1,0:T(8,128)S(1)}, f32[1,256]{1,0:T(1,128)S(1)}) custom-call(f32[1024,256]{1,0:T(8,128)} %power.1, f32[1024,256]{1,0:T(8,128)} %base.1, f32[8,256]{1,0:T(8,128)} %band_low.1, f32[8,256]{1,0:T(8,128)} %band_high.1, bf16[4,256]{1,0:T(4,128)(2,1)} %kernels.1, f32[4,1024]{1,0:T(4,128)} %bitcast.6, s32[1,1024]{1,0:T(1,128)} %bitcast.7, ...), custom_call_target="tpu_custom_call" | custom-call | tf_op jit(solution)/shard_map/pallas_call | solution.py:339
  34.9 1.0 %copy.13 = f32[1024,256]{1,0:T(8,128)} copy(f32[1024,256]{1,0:T(8,128)S(1)} %get-tuple-element.8) | data formatting | bytes 2097152
  35.9 0.6 %copy.14 = f32[256]{0:T(256)} copy(f32[256]{0:T(256)S(1)} %bitcast.5) | data formatting | bytes 2048

commit v2 on v1

--- a/solution.py
+++ b/solution.py
@@ -11,6 +11,9 @@
 ROWS = 128
 MESH = pl.DeviceIdType.MESH
 CODE = 32767.0
+TOP = 4.0
+LEAD = 5
+LAG = 5
 
 
 def split3(value):
@@ -59,6 +62,8 @@
     halo_u,
     code_out,
     code_in,
+    free_out,
+    free_in,
     forward,
     adjoint,
     onehot,
@@ -114,9 +119,10 @@
     ]
 
     def u_copy(it, at, size):
+        source, target = ((packed.at[0], halo_u), (free_out, free_in))[it]
         return pltpu.make_async_remote_copy(
-            src_ref=packed.at[it, pl.ds(at, size)],
-            dst_ref=halo_u.at[it, pl.ds(at, size)],
+            src_ref=source.at[pl.ds(at, size)],
+            dst_ref=target.at[pl.ds(at, size)],
             send_sem=u_send.at[it],
             recv_sem=u_recv.at[it, at // ROWS],
             device_id=right,
@@ -165,14 +171,18 @@
         slots = part_a[it].reshape(nz, 2, 1, steps)
         part_send(it, 1, jnp.sum(slots, axis=0))
 
-    def ratio(it):
+    def ratios(it):
         part_all(it, 1).wait_recv()
         fleet = jnp.sum(part_b[it].reshape(nx, ny, 2, steps), axis=0)
         top = jnp.max(fleet, axis=(0, 1, 2), keepdims=True)[0, 0]
-        mine = part_b[it, y, core]
-        for k in range(1, nx):
-            mine = mine + part_b[it, k * ny + y, core]
-        return mine / top
+
+        def of(block):
+            row = part_b[it, block // 2, lax.rem(block, 2)]
+            for k in range(1, nx):
+                row = row + part_b[it, k * ny + block // 2, lax.rem(block, 2)]
+            return row / top
+
+        return of(tm), of(left[1])
 
     for load in loads:
         load.start()
@@ -211,11 +221,6 @@
     chosen = jnp.where(plans == classes_vm[...], 1.0, 0.0)
     onehot[...] = jnp.concatenate([chosen] * 3, axis=0).T.astype(jnp.bfloat16)
 
-    pl.semaphore_wait(barrier, len(others))
-    send_local(0, sums_first)
-    for at in range(0, count, ROWS):
-        u_copy(0, at, ROWS).start()
-
     at_row = lax.broadcasted_iota(jnp.int32, (steps, steps), 0)
     at_col = lax.broadcasted_iota(jnp.int32, (steps, steps), 1)
     edge = jnp.where(tm > 0, 0, steps)
@@ -229,6 +234,14 @@
         adjoint[place, :steps] = jnp.where(at_row >= at_col, ring, 0.0).astype(jnp.bfloat16)
         adjoint[place, steps:] = jnp.where(at_col - at_row > edge, ring, 0.0).astype(jnp.bfloat16)
 
+    pl.semaphore_wait(barrier, len(others))
+    spots = list(range(0, count, ROWS))
+    for at in spots[:2]:
+        u_copy(0, at, ROWS).start()
+    send_local(0, sums_first)
+    for at in spots[2:LEAD]:
+        u_copy(0, at, ROWS).start()
+
     lows, highs = split3(low_vm[...]), split3(high_vm[...])
     bands = jnp.concatenate(
         [jnp.concatenate([lo, hi], axis=1).astype(jnp.float32) for lo, hi in zip(lows, highs)],
@@ -242,12 +255,10 @@
         under[rows] = value - limits[:, :steps]
         over[rows] = value - limits[:, steps:]
 
-    def excess_and_pull(it, at, size):
-        for part in range(at, at + size, ROWS):
-            u_copy(it, part, ROWS).wait_recv()
-        rows = pl.ds(at, size)
+    def excess_and_pull(it, at, before):
+        rows = pl.ds(at, ROWS)
         col = cols[rows]
-        window = jnp.concatenate([halo_u[it, rows], packed[it, rows]], axis=1)
+        window = jnp.concatenate([before, packed[it, rows]], axis=1)
         hi, lo = over[rows], under[rows]
         parts = []
         for slot in range(zcount):
@@ -264,50 +275,74 @@
         length = jnp.sqrt(jnp.abs(sent) * col[:, 2 * zcount : 2 * zcount + 1])
         code = jnp.round(jnp.where(sent < 0.0, -length, length))
         code_out[it, rows] = jnp.clip(code, -CODE, CODE).astype(jnp.int16)
-        for part in range(at, at + size, ROWS):
-            p_copy(it, part, ROWS).start()
-
-    def free_part(it, at, size, y_now):
-        for part in range(at, at + size, ROWS):
-            p_copy(it, part, ROWS).wait_recv()
-        rows = pl.ds(at, size)
+        p_copy(it, at, ROWS).start()
+
+    def free_part(it, at, y_now):
+        p_copy(it, at, ROWS).wait_recv()
+        rows = pl.ds(at, ROWS)
         code = code_in[it, rows].astype(jnp.float32)
         scale = cols[rows][:, 2 * zcount + 1 : 2 * zcount + 2]
         pull = own[rows] + code * jnp.abs(code) * scale
         return u_now[rows] - 0.5 * (y_now - pull)
 
+    reach = TOP + 0.5
+    fine = 2.0 * CODE / reach
     y_now = duals_vm[...]
-    places = [(0, 256), (256, 256), (512, 256), (768, 128), (896, 128)]
-    assert places[-1][0] + places[-1][1] == count
-
-    excess_and_pull(0, *places[0])
-    send_pair(0)
-    for place in places[1:]:
-        excess_and_pull(0, *place)
-    now = ratio(0)
-    share = 0.5 * now
-    sums = jnp.zeros((8, steps), jnp.float32)
-    for at in range(0, count, ROWS):
+
+    def open_first(at):
+        u_copy(0, at, ROWS).wait_recv()
+        excess_and_pull(0, at, halo_u[pl.ds(at, ROWS)])
+
+    def send_free(at):
         rows = pl.ds(at, ROWS)
-        value = jnp.clip(free_part(0, at, ROWS, y_now) - share, 0.0, 4.0)
+        value = free_part(0, at, y_now)
+        u_now[rows] = value
+        code = jnp.round(jnp.clip(value, 0.0, reach) * fine - CODE)
+        free_out[rows] = code.astype(jnp.int16)
+        u_copy(1, at, ROWS).start()
+
+    def settle(at, share):
+        rows = pl.ds(at, ROWS)
+        value = jnp.clip(u_now[rows] - share, 0.0, TOP)
         u_now[rows] = value
         packed[1, rows] = value.astype(jnp.bfloat16)
-        sums = sums + fold(value)
-        u_copy(1, at, ROWS).start()
+        return fold(value)
+
+    def open_second(at, share_left):
+        u_copy(1, at, ROWS).wait_recv()
+        code = free_in[pl.ds(at, ROWS)].astype(jnp.float32)
+        before = jnp.clip((code + CODE) * (1.0 / fine) - share_left, 0.0, TOP)
+        excess_and_pull(1, at, before.astype(jnp.bfloat16))
+
+    for i, at in enumerate(spots):
+        open_first(at)
+        if i + LEAD < copies:
+            u_copy(0, spots[i + LEAD], ROWS).start()
+        if i == 2:
+            send_pair(0)
+        if i >= LAG:
+            send_free(spots[i - LAG])
+    send_free(spots[copies - LAG])
+    now, now_left = ratios(0)
+    share, share_left = 0.5 * now, 0.5 * now_left
+    sums = jnp.zeros((8, steps), jnp.float32)
+    for at in spots[copies - LAG + 1 :]:
+        send_free(at)
+        sums = sums + settle(at, share)
+    for at in spots[: copies - LAG + 1]:
+        sums = sums + settle(at, share)
     send_local(1, sums)
     y_now = y_now + 1.0 * (now - 0.5)
 
-    excess_and_pull(1, *places[0])
-    excess_and_pull(1, *places[1])
+    for at in spots:
+        open_second(at, share_left)
     send_pair(1)
-    for place in places[2:]:
-        excess_and_pull(1, *place)
-    for at, size in places:
-        own[pl.ds(at, size)] = free_part(1, at, size, y_now)
-    now = ratio(1)
+    for at in spots:
+        own[pl.ds(at, ROWS)] = free_part(1, at, y_now)
+    now, _ = ratios(1)
     share = 0.5 * now
     duals_out[...] = y_now + 1.0 * (now - 0.5)
-    out[...] = jnp.clip(own[...] - share, 0.0, 4.0)
+    out[...] = jnp.clip(own[...] - share, 0.0, TOP)
 
     for it in range(ITERS):
         u_copy(it, 0, count).wait_send()
@@ -351,9 +386,11 @@
             whole,
             whole,
             pltpu.VMEM((ITERS, count, steps), bf16),
-            pltpu.VMEM((ITERS, count, steps), bf16),
+            pltpu.VMEM((count, steps), bf16),
             pltpu.VMEM((ITERS, count, steps), jnp.int16),
             pltpu.VMEM((ITERS, count, steps), jnp.int16),
+            pltpu.VMEM((count, steps), jnp.int16),
+            pltpu.VMEM((count, steps), jnp.int16),
             pltpu.VMEM((2 * steps, zcount * steps), bf16),
             pltpu.VMEM((zcount * steps, 2 * steps), bf16),
             pltpu.VMEM((count, 3 * nsched), bf16),

time: 36.5 us -> 35.3 us (0.967)
  Pallas kernels: 34.3 us -> 33 us
    pallas_call x1, Pallas kernels: 34.3 us -> 33 us  [body(): pl.pallas_call(functools.partial(kernel, nz, nx, nt), out_shape=(jax.Shap...]
where the time goes in v2:
time: 35.3 us; the launch traced here: 35.2 us
  Pallas kernels  33 us (93%)
  local copies, waits for them, and re-layouts  1.54 us (4%)
  between operations  0.64 us (2%)
    pallas_call x1, Pallas kernels, body(): pl.pallas_call(functools.partial(kernel, nz, nx, nt), out_shape=(jax.Shap...  33 us
    unnamed x2, local copies, waits for them, and re-layouts  1.54 us

profile of v2, /device:TPU:1, one launch (start us, length us, event | category | flops | bytes accessed | tf_op | source)
XLA Modules:
  0.0 35.2 jit_solution(14380951125078104572)
XLA Ops:
  0.6 33.0 %shard_map.104 = (f32[1024,256]{1,0:T(8,128)S(1)}, f32[1,256]{1,0:T(1,128)S(1)}) custom-call(f32[1024,256]{1,0:T(8,128)} %power.1, f32[1024,256]{1,0:T(8,128)} %base.1, f32[8,256]{1,0:T(8,128)} %band_low.1, f32[8,256]{1,0:T(8,128)} %band_high.1, bf16[4,256]{1,0:T(4,128)(2,1)} %kernels.1, f32[4,1024]{1,0:T(4,128)} %bitcast.6, s32[1,1024]{1,0:T(1,128)} %bitcast.7, ...), custom_call_target="tpu_custom_call" | custom-call | tf_op jit(solution)/shard_map/pallas_call | solution.py:374
  33.7 1.0 %copy.13 = f32[1024,256]{1,0:T(8,128)} copy(f32[1024,256]{1,0:T(8,128)S(1)} %get-tuple-element.8) | data formatting | bytes 2097152
  34.6 0.6 %copy.14 = f32[256]{0:T(256)} copy(f32[256]{0:T(256)S(1)} %bitcast.5) | data formatting | bytes 2048

commit v3 on v2

--- a/solution.py
+++ b/solution.py
@@ -12,7 +12,9 @@
 MESH = pl.DeviceIdType.MESH
 CODE = 32767.0
 TOP = 4.0
+PIECES = 4
 LEAD = 5
+LATE = 1
 LAG = 5
 
 
@@ -47,6 +49,7 @@
     duals,
     out,
     duals_out,
+    share_out,
     low_vm,
     high_vm,
     kern_vm,
@@ -68,8 +71,10 @@
     adjoint,
     onehot,
     cols,
-    part_a,
-    part_b,
+    part_xt,
+    part_z,
+    part_zc,
+    part_xy,
     load_sem,
     u_send,
     u_recv,
@@ -89,15 +94,25 @@
     right = (bld, lax.rem(tm + 1, nt))
     left = (bld, lax.rem(tm + nt - 1, nt))
 
-    far_a = spread([2 * around(k // 2, nz) + k % 2 for k in range(2 * nz)])
-    far_b = spread([around(k // ny, nx) + around(k % ny, ny) for k in range(nx * ny)])
-    peers_a = [
-        (x * nz + lax.rem(z + k // 2, nz), 2 * y + lax.rem(core + k % 2, 2)) for k in far_a
+    def hops(k):
+        return around(k // ny, nx) + around(k % ny, ny)
+
+    far_xt = spread([2 * around(k // nt, nx) + around(k % nt, nt) for k in range(nx * nt)])
+    far_z = spread([around(k, nz) for k in range(nz)])
+    far_zc = spread([2 * around(k // 2, nz) + k % 2 for k in range(2 * nz)])
+    far_xy = spread([hops(k) for k in range(nx * ny)])
+    peers_xt = [(lax.rem(x + k // nt, nx) * nz + z, lax.rem(tm + k % nt, nt)) for k in far_xt]
+    peers_z = [(x * nz + lax.rem(z + k, nz), tm) for k in far_z]
+    peers_zc = [
+        (x * nz + lax.rem(z + k // 2, nz), 2 * y + lax.rem(core + k % 2, 2)) for k in far_zc
     ]
-    peers_b = [
-        (lax.rem(x + k // ny, nx) * nz + z, 2 * lax.rem(y + k % ny, ny) + core) for k in far_b
+    peers_xy = [
+        (lax.rem(x + k // ny, nx) * nz + z, 2 * lax.rem(y + k % ny, ny) + core) for k in far_xy
     ]
-    stages = ((part_a, peers_a, 2 * z + core), (part_b, peers_b, x * ny + y))
+    stages = (
+        ((part_zc, peers_zc, 2 * z + core), (part_xy, peers_xy, x * ny + y)),
+        ((part_xt, peers_xt, x * nt + tm), (part_z, peers_z, z)),
+    )
 
     small = (
         (gains, gains_vm),
@@ -109,12 +124,16 @@
         (duals, duals_vm),
     )
     half = count // 2
+    piece = count // PIECES
+    pieces = [
+        pltpu.make_async_copy(
+            power.at[pl.ds(i * piece, piece)], u_now.at[pl.ds(i * piece, piece)], load_sem.at[i]
+        )
+        for i in range(PIECES)
+    ]
+    base_load = pltpu.make_async_copy(base, under, load_sem.at[PIECES])
     loads = [
-        pltpu.make_async_copy(power.at[pl.ds(0, half)], u_now.at[pl.ds(0, half)], load_sem.at[0]),
-        pltpu.make_async_copy(power.at[pl.ds(half, half)], u_now.at[pl.ds(half, half)], load_sem.at[1]),
-        pltpu.make_async_copy(base, under, load_sem.at[2]),
-    ] + [
-        pltpu.make_async_copy(source, target, load_sem.at[3 + i])
+        pltpu.make_async_copy(source, target, load_sem.at[PIECES + 1 + i])
         for i, (source, target) in enumerate(small)
     ]
 
@@ -140,12 +159,12 @@
         )
 
     def part_send(it, stage, value):
-        buf, peers, mine = stages[stage]
-        buf[it, mine] = value
+        buf, peers, mine = stages[it][stage]
+        buf[mine] = value
         for peer in peers:
             pltpu.make_async_remote_copy(
-                src_ref=buf.at[it, mine],
-                dst_ref=buf.at[it, mine],
+                src_ref=buf.at[mine],
+                dst_ref=buf.at[mine],
                 send_sem=r_send.at[it, stage],
                 recv_sem=r_recv.at[it, stage],
                 device_id=peer,
@@ -153,10 +172,10 @@
             ).start()
 
     def part_all(it, stage):
-        buf, peers, _ = stages[stage]
+        buf, peers, _ = stages[it][stage]
         return pltpu.make_async_remote_copy(
-            src_ref=buf.at[it, pl.ds(0, len(peers))],
-            dst_ref=buf.at[it, pl.ds(0, len(peers))],
+            src_ref=buf.at[pl.ds(0, len(peers))],
+            dst_ref=buf.at[pl.ds(0, len(peers))],
             send_sem=r_send.at[it, stage],
             recv_sem=r_recv.at[it, stage],
             device_id=peers[0],
@@ -166,43 +185,60 @@
     def send_local(it, sums):
         part_send(it, 0, jnp.sum(sums, axis=0, keepdims=True))
 
-    def send_pair(it):
+    def send_rest(it):
         part_all(it, 0).wait_recv()
-        slots = part_a[it].reshape(nz, 2, 1, steps)
-        part_send(it, 1, jnp.sum(slots, axis=0))
+        buf = stages[it][0][0]
+        members, each = ((nz, 2), (nx, nt))[it]
+        part_send(it, 1, jnp.sum(buf[...].reshape(members, each, 1, steps), axis=0))
 
     def ratios(it):
         part_all(it, 1).wait_recv()
-        fleet = jnp.sum(part_b[it].reshape(nx, ny, 2, steps), axis=0)
-        top = jnp.max(fleet, axis=(0, 1, 2), keepdims=True)[0, 0]
+        buf = stages[it][1][0]
+        if it == 1:
+            fleet = jnp.sum(buf[...], axis=0)
+            top = jnp.max(fleet, axis=(0, 1, 2), keepdims=True)[0]
+        else:
+            fleet = jnp.sum(buf[...].reshape(nx, ny, 2, steps), axis=0)
+            top = jnp.max(fleet, axis=(0, 1, 2), keepdims=True)[0, 0]
 
         def of(block):
-            row = part_b[it, block // 2, lax.rem(block, 2)]
-            for k in range(1, nx):
-                row = row + part_b[it, k * ny + block // 2, lax.rem(block, 2)]
+            if it == 1:
+                picks = [buf[k, block] for k in range(nz)]
+            else:
+                picks = [buf[k * ny + block // 2, lax.rem(block, 2)] for k in range(nx)]
+            row = picks[0]
+            for pick in picks[1:]:
+                row = row + pick
             return row / top
 
         return of(tm), of(left[1])
 
-    for load in loads:
+    for load in pieces + loads + [base_load]:
         load.start()
 
     barrier = pltpu.get_barrier_semaphore()
-    others = peers_a + peers_b + [left, right]
+    others = peers_xt + [p for k, p in zip(far_zc, peers_zc) if k > 1]
     for peer in others:
         pl.semaphore_signal(barrier, inc=1, device_id=peer, device_id_type=MESH)
 
     def fold(value):
         return jnp.sum(value.reshape(value.shape[0] // 8, 8, steps), axis=0)
 
+    spots = list(range(0, count, ROWS))
     sums = jnp.zeros((8, steps), jnp.float32)
-    for i in range(2):
-        loads[i].wait()
-        value = u_now[pl.ds(i * half, half)]
-        packed[0, pl.ds(i * half, half)] = value.astype(jnp.bfloat16)
+    for i, load in enumerate(pieces):
+        load.wait()
+        rows = pl.ds(i * piece, piece)
+        value = u_now[rows]
+        packed[0, rows] = value.astype(jnp.bfloat16)
+        if i == 0:
+            pl.semaphore_wait(barrier, len(others))
+        for at in spots[:LEAD]:
+            if at // piece == i:
+                u_copy(0, at, ROWS).start()
         sums = sums + fold(value)
-    sums_first = sums
-    for load in loads[3:]:
+    send_local(0, sums)
+    for load in loads:
         load.wait()
 
     kern = kern_vm[...].astype(jnp.float32)
@@ -234,20 +270,12 @@
         adjoint[place, :steps] = jnp.where(at_row >= at_col, ring, 0.0).astype(jnp.bfloat16)
         adjoint[place, steps:] = jnp.where(at_col - at_row > edge, ring, 0.0).astype(jnp.bfloat16)
 
-    pl.semaphore_wait(barrier, len(others))
-    spots = list(range(0, count, ROWS))
-    for at in spots[:2]:
-        u_copy(0, at, ROWS).start()
-    send_local(0, sums_first)
-    for at in spots[2:LEAD]:
-        u_copy(0, at, ROWS).start()
-
     lows, highs = split3(low_vm[...]), split3(high_vm[...])
     bands = jnp.concatenate(
         [jnp.concatenate([lo, hi], axis=1).astype(jnp.float32) for lo, hi in zip(lows, highs)],
         axis=0,
     ).astype(jnp.bfloat16)
-    loads[2].wait()
+    base_load.wait()
     for at in range(0, count, half):
         rows = pl.ds(at, half)
         limits = jnp.dot(onehot[rows], bands, preferred_element_type=jnp.float32)
@@ -299,7 +327,8 @@
         u_now[rows] = value
         code = jnp.round(jnp.clip(value, 0.0, reach) * fine - CODE)
         free_out[rows] = code.astype(jnp.int16)
-        u_copy(1, at, ROWS).start()
+        if at < spots[copies - LATE]:
+            u_copy(1, at, ROWS).start()
 
     def settle(at, share):
         rows = pl.ds(at, ROWS)
@@ -319,30 +348,31 @@
         if i + LEAD < copies:
             u_copy(0, spots[i + LEAD], ROWS).start()
         if i == 2:
-            send_pair(0)
+            send_rest(0)
         if i >= LAG:
             send_free(spots[i - LAG])
     send_free(spots[copies - LAG])
     now, now_left = ratios(0)
     share, share_left = 0.5 * now, 0.5 * now_left
     sums = jnp.zeros((8, steps), jnp.float32)
+    for at in spots[: copies - LAG + 1]:
+        sums = sums + settle(at, share)
     for at in spots[copies - LAG + 1 :]:
         send_free(at)
         sums = sums + settle(at, share)
-    for at in spots[: copies - LAG + 1]:
-        sums = sums + settle(at, share)
     send_local(1, sums)
+    for at in spots[copies - LATE :]:
+        u_copy(1, at, ROWS).start()
     y_now = y_now + 1.0 * (now - 0.5)
 
     for at in spots:
         open_second(at, share_left)
-    send_pair(1)
+    send_rest(1)
     for at in spots:
-        own[pl.ds(at, ROWS)] = free_part(1, at, y_now)
+        out[pl.ds(at, ROWS)] = free_part(1, at, y_now)
     now, _ = ratios(1)
-    share = 0.5 * now
     duals_out[...] = y_now + 1.0 * (now - 0.5)
-    out[...] = jnp.clip(own[...] - share, 0.0, TOP)
+    share_out[...] = 0.5 * now
 
     for it in range(ITERS):
         u_copy(it, 0, count).wait_send()
@@ -371,14 +401,15 @@
         classes[None, :],
         duals[None, :],
     )
-    out, duals_out = pl.pallas_call(
+    free, duals_out, share = pl.pallas_call(
         functools.partial(kernel, nz, nx, nt),
         out_shape=(
             jax.ShapeDtypeStruct((count, steps), f32),
             jax.ShapeDtypeStruct((1, steps), f32),
+            jax.ShapeDtypeStruct((1, steps), f32),
         ),
         in_specs=[hbm] * len(args),
-        out_specs=(vmem, vmem),
+        out_specs=(vmem, vmem, vmem),
         scratch_shapes=[pltpu.VMEM(arg.shape, arg.dtype) for arg in args[2:]]
         + [
             whole,
@@ -395,9 +426,11 @@
             pltpu.VMEM((zcount * steps, 2 * steps), bf16),
             pltpu.VMEM((count, 3 * nsched), bf16),
             pltpu.VMEM((count, 16), f32),
-            pltpu.VMEM((ITERS, 2 * nz, 1, steps), f32),
-            pltpu.VMEM((ITERS, nx * nt // 2, 2, 1, steps), f32),
-            pltpu.SemaphoreType.DMA((3 + len(args) - 2,)),
+            pltpu.VMEM((nx * nt, 1, steps), f32),
+            pltpu.VMEM((nz, nt, 1, steps), f32),
+            pltpu.VMEM((2 * nz, 1, steps), f32),
+            pltpu.VMEM((nx * nt // 2, 2, 1, steps), f32),
+            pltpu.SemaphoreType.DMA((PIECES + 1 + len(args) - 2,)),
             pltpu.SemaphoreType.DMA((ITERS,)),
             pltpu.SemaphoreType.DMA((ITERS, copies)),
             pltpu.SemaphoreType.DMA((ITERS,)),
@@ -409,7 +442,7 @@
             collective_id=0, has_side_effects=True, vmem_limit_bytes=40 * 1024 * 1024
         ),
     )(*[pltpu.with_memory_space_constraint(arg, pltpu.HBM) for arg in args])
-    return out, duals_out[0]
+    return jnp.clip(free - share, 0.0, TOP), duals_out[0]
 
 
 def solution(mesh):

time: 35.3 us -> 34.7 us (0.983)
  other arithmetic: 0 us -> 1.04 us
  local copies, waits for them, and re-layouts: 1.54 us -> 0.56 us
  Pallas kernels: 33 us -> 32.4 us
    min x0 -> x1, other arithmetic: none -> 1.04 us  [body(): return (jnp.clip(free - share, 0.0, TOP), duals_out[0])]
    unnamed x2 -> x1, local copies, waits for them, and re-layouts: 1.54 us -> 0.56 us
    pallas_call x1, Pallas kernels: 33 us -> 32.4 us  [body(): pl.pallas_call(functools.partial(kernel, nz, nx, nt), out_shape=(jax.Shap...]
where the time goes in v3:
time: 34.7 us; the launch traced here: 34.6 us
  Pallas kernels  32.4 us (93%)
  other arithmetic  1.04 us (3%)
  between operations  0.64 us (2%)
  local copies, waits for them, and re-layouts  0.56 us (2%)
    pallas_call x1, Pallas kernels, body(): pl.pallas_call(functools.partial(kernel, nz, nx, nt), out_shape=(jax.Shap...  32.4 us
    min x1, other arithmetic, body(): return (jnp.clip(free - share, 0.0, TOP), duals_out[0])  1.04 us

profile of v3, /device:TPU:1, one launch (start us, length us, event | category | flops | bytes accessed | tf_op | source)
XLA Modules:
  0.0 34.6 jit_solution(4688464624915955715)
XLA Ops:
  0.6 32.4 %shard_map.104 = (f32[1024,256]{1,0:T(8,128)S(1)}, f32[1,256]{1,0:T(1,128)S(1)}, f32[1,256]{1,0:T(1,128)S(1)}) custom-call(f32[1024,256]{1,0:T(8,128)} %power.1, f32[1024,256]{1,0:T(8,128)} %base.1, f32[8,256]{1,0:T(8,128)} %band_low.1, f32[8,256]{1,0:T(8,128)} %band_high.1, bf16[4,256]{1,0:T(4,128)(2,1)} %kernels.1, f32[4,1024]{1,0:T(4,128)} %bitcast.8, ...), custom_call_target="tpu_custom_call" | custom-call | tf_op jit(solution)/shard_map/pallas_call | solution.py:404
  33.0 1.0 %subtract_clamp_fusion = f32[1024,256]{1,0:T(8,128)} fusion(f32[1024,256]{1,0:T(8,128)S(1)} %get-tuple-element.5, f32[256]{0:T(256)S(1)} %bitcast.6), kind=kLoop, calls=%fused_computation | loop fusion | flops 524288 | bytes 2098176 | tf_op jit(solution)/shard_map/jit(clip)/min | solution.py:445
  34.0 0.6 %copy.12 = f32[256]{0:T(256)} copy(f32[256]{0:T(256)S(1)} %bitcast.7) | data formatting | bytes 2048

commit v4 on v3

--- a/solution.py
+++ b/solution.py
@@ -283,8 +283,8 @@
         under[rows] = value - limits[:, :steps]
         over[rows] = value - limits[:, steps:]
 
-    def excess_and_pull(it, at, before):
-        rows = pl.ds(at, ROWS)
+    def excess_and_pull(it, at, before, size=ROWS):
+        rows = pl.ds(at, size)
         col = cols[rows]
         window = jnp.concatenate([before, packed[it, rows]], axis=1)
         hi, lo = over[rows], under[rows]
@@ -303,7 +303,8 @@
         length = jnp.sqrt(jnp.abs(sent) * col[:, 2 * zcount : 2 * zcount + 1])
         code = jnp.round(jnp.where(sent < 0.0, -length, length))
         code_out[it, rows] = jnp.clip(code, -CODE, CODE).astype(jnp.int16)
-        p_copy(it, at, ROWS).start()
+        for part in range(at, at + size, ROWS):
+            p_copy(it, part, ROWS).start()
 
     def free_part(it, at, y_now):
         p_copy(it, at, ROWS).wait_recv()
@@ -337,11 +338,12 @@
         packed[1, rows] = value.astype(jnp.bfloat16)
         return fold(value)
 
-    def open_second(at, share_left):
-        u_copy(1, at, ROWS).wait_recv()
-        code = free_in[pl.ds(at, ROWS)].astype(jnp.float32)
+    def open_second(at, size, share_left):
+        for part in range(at, at + size, ROWS):
+            u_copy(1, part, ROWS).wait_recv()
+        code = free_in[pl.ds(at, size)].astype(jnp.float32)
         before = jnp.clip((code + CODE) * (1.0 / fine) - share_left, 0.0, TOP)
-        excess_and_pull(1, at, before.astype(jnp.bfloat16))
+        excess_and_pull(1, at, before.astype(jnp.bfloat16), size)
 
     for i, at in enumerate(spots):
         open_first(at)
@@ -365,8 +367,11 @@
         u_copy(1, at, ROWS).start()
     y_now = y_now + 1.0 * (now - 0.5)
 
-    for at in spots:
-        open_second(at, share_left)
+    pairs = spots[: copies - 2 : 2]
+    for at in pairs:
+        open_second(at, 2 * ROWS, share_left)
+    for at in spots[copies - 2 :]:
+        open_second(at, ROWS, share_left)
     send_rest(1)
     for at in spots:
         out[pl.ds(at, ROWS)] = free_part(1, at, y_now)

time: 34.7 us -> 34.2 us (0.986)
  Pallas kernels: 32.4 us -> 31.8 us
    pallas_call x1, Pallas kernels: 32.4 us -> 31.8 us  [body(): pl.pallas_call(functools.partial(kernel, nz, nx, nt), out_shape=(jax.Shap...]
where the time goes in v4:
time: 34.2 us; the launch traced here: 34.1 us
  Pallas kernels  31.8 us (93%)
  other arithmetic  1.04 us (3%)
  between operations  0.64 us (2%)
  local copies, waits for them, and re-layouts  0.56 us (2%)
    pallas_call x1, Pallas kernels, body(): pl.pallas_call(functools.partial(kernel, nz, nx, nt), out_shape=(jax.Shap...  31.8 us
    min x1, other arithmetic, body(): return (jnp.clip(free - share, 0.0, TOP), duals_out[0])  1.04 us

profile of v4, /device:TPU:1, one launch (start us, length us, event | category | flops | bytes accessed | tf_op | source)
XLA Modules:
  0.0 34.1 jit_solution(7974497983320232532)
XLA Ops:
  0.6 31.8 %shard_map.104 = (f32[1024,256]{1,0:T(8,128)S(1)}, f32[1,256]{1,0:T(1,128)S(1)}, f32[1,256]{1,0:T(1,128)S(1)}) custom-call(f32[1024,256]{1,0:T(8,128)} %power.1, f32[1024,256]{1,0:T(8,128)} %base.1, f32[8,256]{1,0:T(8,128)} %band_low.1, f32[8,256]{1,0:T(8,128)} %band_high.1, bf16[4,256]{1,0:T(4,128)(2,1)} %kernels.1, f32[4,1024]{1,0:T(4,128)} %bitcast.8, ...), custom_call_target="tpu_custom_call" | custom-call | tf_op jit(solution)/shard_map/pallas_call | solution.py:409
  32.5 1.0 %subtract_clamp_fusion = f32[1024,256]{1,0:T(8,128)} fusion(f32[1024,256]{1,0:T(8,128)S(1)} %get-tuple-element.5, f32[256]{0:T(256)S(1)} %bitcast.6), kind=kLoop, calls=%fused_computation | loop fusion | flops 524288 | bytes 2098176 | tf_op jit(solution)/shard_map/jit(clip)/min | solution.py:450
  33.5 0.6 %copy.12 = f32[256]{0:T(256)} copy(f32[256]{0:T(256)S(1)} %bitcast.7) | data formatting | bytes 2048
